TPU v7x, 32 devices: a whole 2x2x4 slice. The times are simulated.
32 devices in a mesh: seq: 8 (over z, x), slide: 4 (over y, core).
Axes of the slice: x: 2, y: 2, z: 4, core: 2. Of those that a mesh axis runs over, the one named last changes fastest.
Arguments:
- tokens: bfloat16 [4, 4096, 768], P('slide', 'seq'), may hold values from -6 to 6
- qkv_weight: bfloat16 [768, 2304], replicated, may hold values from -0.21875 to 0.21875
- out_weight: bfloat16 [768, 768], replicated, may hold values from -3 to 3
- up_weight: bfloat16 [768, 3072], replicated, may hold values from -0.21875 to 0.21875
- down_weight: bfloat16 [3072, 768], replicated, may hold values from -0.109375 to 0.109375
- norm1_gain: float32 [768], replicated, may hold values from 0.5 to 1.5
- norm1_bias: float32 [768], replicated, may hold values from -2 to 2
- norm2_gain: float32 [768], replicated, may hold values from 0.5 to 1.5
- norm2_bias: float32 [768], replicated, may hold values from -2 to 2
- visible: int32 [4], P('slide'), may hold values from 2048 to 4096, as said below
- cotangent: bfloat16 [4, 4096, 768], P('slide', 'seq'), may hold values from -6 to 6
Outputs:
- mixed: bfloat16 [4, 4096, 768], P('slide', 'seq')
- tokens_grad: bfloat16 [4, 4096, 768], P('slide', 'seq')
- qkv_grad: float32 [768, 2304], P('seq')
- out_grad: float32 [768, 768], P('seq')
- up_grad: float32 [768, 3072], P('seq')
- down_grad: float32 [3072, 768], P('seq')
- norm1_gain_grad: float32 [768], replicated
- norm1_bias_grad: float32 [768], replicated
- norm2_gain_grad: float32 [768], replicated
- norm2_bias_grad: float32 [768], replicated
Inputs may be any that keep to these rules, and one draw needn't show every extreme that they name: Entry b counts the leading rows of slide b that hold visible tiles; every row after them is padding. Some slide is full (4096 rows) and another holds exactly 2048.
All inputs are finite; a program needn't handle non-finite values.
Results may differ from a plain program's by a relative error of at most 0.013.
Values may be sent and summed in bfloat16 or wider, within the bound.
A program may use at most 256 MiB of HBM per device.

v0:
```python
import functools

import jax
import jax.numpy as jnp
from jax import lax
from jax.experimental import pallas as pl
from jax.experimental.pallas import tpu as pltpu
from jax.sharding import PartitionSpec as P

HEADS = 16
HEAD_WIDTH = 48
SEG = 512
QB = 512
DILATION_STEP = 16


epsilon = 1e-05


def layer_norm(values, norm_gain, norm_shift):
    average = jnp.mean(values, axis=-1, keepdims=True)
    centered = values - average
    variance = jnp.mean(centered * centered, axis=-1, keepdims=True)
    return centered * lax.rsqrt(variance + epsilon) * norm_gain + norm_shift


def exact_gelu(values):
    return jax.nn.gelu(values, approximate=False)


def block_scores(query_block, seg_keys, seg_valid, distant_keys, distant_valid):
    nearby_scores = jnp.einsum(
        "iyo,uyo->yiu", query_block, seg_keys, preferred_element_type=jnp.float32
    )
    nearby_scores = jnp.where(seg_valid[None, None, :], nearby_scores, -1000000000.0)
    far_scores = jnp.einsum(
        "iyo,uyo->yiu",
        query_block[::DILATION_STEP],
        distant_keys,
        preferred_element_type=jnp.float32,
    )
    far_scores = jnp.where(distant_valid[None, None, :], far_scores, -1000000000.0)
    return (nearby_scores, far_scores)


def block_forward(
    query_block, seg_keys, seg_values, seg_valid, distant_keys, distant_values, distant_valid
):
    nearby_scores, far_scores = block_scores(
        query_block, seg_keys, seg_valid, distant_keys, distant_valid
    )
    head_number = nearby_scores.shape[0]
    row_number = nearby_scores.shape[1]
    chosen_count = row_number // DILATION_STEP
    maximum_table = jnp.max(nearby_scores, axis=-1).reshape(
        head_number, chosen_count, DILATION_STEP
    )
    combined_top = jnp.maximum(maximum_table[:, :, 0], jnp.max(far_scores, axis=-1))
    row_maximum = maximum_table.at[:, :, 0].set(combined_top).reshape(head_number, row_number)
    nearby_exponent = jnp.exp(nearby_scores - row_maximum[:, :, None])
    far_exp = jnp.exp(far_scores - combined_top[:, :, None])
    exponent_sums = jnp.sum(nearby_exponent, axis=-1).reshape(
        head_number, chosen_count, DILATION_STEP
    )
    combined_total = exponent_sums[:, :, 0] + jnp.sum(far_exp, axis=-1)
    row_sum_total = exponent_sums.at[:, :, 0].set(combined_total).reshape(head_number, row_number)
    local_weights = (nearby_exponent / row_sum_total[:, :, None]).astype(jnp.bfloat16)
    far_weights = (far_exp / combined_total[:, :, None]).astype(jnp.bfloat16)
    attended_rows = jnp.einsum(
        "hqk,khd->qhd", local_weights, seg_values, preferred_element_type=jnp.float32
    )
    distant_attended = jnp.einsum(
        "hqk,khd->qhd", far_weights, distant_values, preferred_element_type=jnp.float32
    )
    attended_rows = (
        attended_rows.reshape(chosen_count, DILATION_STEP, head_number, HEAD_WIDTH)
        .at[:, 0]
        .add(distant_attended)
    )
    return (attended_rows.reshape(row_number, head_number, HEAD_WIDTH), row_maximum, row_sum_total)


def block_backward(
    query_block,
    seg_keys,
    seg_values,
    seg_valid,
    distant_keys,
    distant_values,
    distant_valid,
    gradient_block,
    row_maximum,
    row_sum_total,
):
    nearby_scores, far_scores = block_scores(
        query_block, seg_keys, seg_valid, distant_keys, distant_valid
    )
    head_number = row_maximum.shape[0]
    row_number = row_maximum.shape[1]
    chosen_count = row_number // DILATION_STEP
    combined_top = row_maximum.reshape(head_number, chosen_count, DILATION_STEP)[:, :, 0]
    combined_total = row_sum_total.reshape(head_number, chosen_count, DILATION_STEP)[:, :, 0]
    nearby_probability = (
        jnp.exp(nearby_scores - row_maximum[:, :, None]) / row_sum_total[:, :, None]
    )
    far_prob = jnp.exp(far_scores - combined_top[:, :, None]) / combined_total[:, :, None]
    local_weights = nearby_probability.astype(jnp.bfloat16)
    gradient_sampled = gradient_block[::DILATION_STEP]
    value_grad = jnp.einsum(
        "mns,nmg->smg", local_weights, gradient_block, preferred_element_type=jnp.float32
    )
    nearby_dots = jnp.einsum(
        "iyo,uyo->yiu", gradient_block, seg_values, preferred_element_type=jnp.float32
    )
    far_dots = jnp.einsum(
        "iyo,uyo->yiu", gradient_sampled, distant_values, preferred_element_type=jnp.float32
    )
    delta_table = jnp.sum(nearby_probability * nearby_dots, axis=-1).reshape(
        head_number, chosen_count, DILATION_STEP
    )
    joint_delta = delta_table[:, :, 0] + jnp.sum(far_prob * far_dots, axis=-1)
    row_delta = delta_table.at[:, :, 0].set(joint_delta).reshape(head_number, row_number)
    local_slope = (nearby_probability * (nearby_dots - row_delta[:, :, None])).astype(jnp.bfloat16)
    distant_slope = (far_prob * (far_dots - joint_delta[:, :, None])).astype(jnp.bfloat16)
    query_gradient = jnp.einsum(
        "hqk,khd->qhd", local_slope, seg_keys, preferred_element_type=jnp.float32
    )
    distant_query = jnp.einsum(
        "hqk,khd->qhd", distant_slope, distant_keys, preferred_element_type=jnp.float32
    )
    query_gradient = (
        query_gradient.reshape(chosen_count, DILATION_STEP, head_number, HEAD_WIDTH)
        .at[:, 0]
        .add(distant_query)
    )
    key_grad = jnp.einsum(
        "mns,nmg->smg", local_slope, query_block, preferred_element_type=jnp.float32
    )
    far_weights = far_prob.astype(jnp.bfloat16)
    far_value_grad = jnp.einsum(
        "mns,nmg->smg", far_weights, gradient_sampled, preferred_element_type=jnp.float32
    )
    far_key_grad = jnp.einsum(
        "mns,nmg->smg",
        distant_slope,
        query_block[::DILATION_STEP],
        preferred_element_type=jnp.float32,
    )
    return (
        query_gradient.reshape(row_number, head_number, HEAD_WIDTH),
        key_grad,
        value_grad,
        far_key_grad,
        far_value_grad,
    )


def plain_device(
    tokens,
    qkv_weight,
    out_weight,
    up_weight,
    down_weight,
    norm1_gain,
    norm1_bias,
    norm2_gain,
    norm2_bias,
    visible,
    cotangent,
):
    row_number = tokens.shape[1]
    embedding_width = tokens.shape[2]
    query_scale = HEAD_WIDTH ** (-0.5)
    first_row = lax.axis_index("seq") * row_number
    positions = first_row + jnp.arange(row_number, dtype=jnp.int32)
    row_validity = positions < visible[0]
    inputs = tokens[0].astype(jnp.float32)
    norm_one, pull_one = jax.vjp(layer_norm, inputs, norm1_gain, norm1_bias)
    normed = norm_one.astype(jnp.bfloat16)
    projected = jnp.dot(normed, qkv_weight, preferred_element_type=jnp.float32)
    query_rows = (
        (projected[:, :embedding_width] * query_scale)
        .astype(jnp.bfloat16)
        .reshape(row_number, HEADS, HEAD_WIDTH)
    )
    flat_keys = projected[:, embedding_width : 2 * embedding_width].astype(jnp.bfloat16)
    flat_values = projected[:, 2 * embedding_width :].astype(jnp.bfloat16)
    key_matrix = flat_keys.reshape(row_number, HEADS, HEAD_WIDTH)
    value_matrix = flat_values.reshape(row_number, HEADS, HEAD_WIDTH)
    gathered_keys, gathered_values = (
        lax.all_gather(flat_keys[::DILATION_STEP], "seq", axis=0, tiled=True),
        lax.all_gather(flat_values[::DILATION_STEP], "seq", axis=0, tiled=True),
    )
    distant_count = gathered_keys.shape[0]
    distant_valid = jnp.arange(distant_count, dtype=jnp.int32) * DILATION_STEP < visible[0]
    distant_keys = gathered_keys.reshape(distant_count, HEADS, HEAD_WIDTH)
    distant_values = gathered_values.reshape(distant_count, HEADS, HEAD_WIDTH)
    per_segment = SEG // QB
    attended_rows, row_maximum, row_sum_total = block_forward(
        query_rows,
        key_matrix,
        value_matrix,
        row_validity,
        distant_keys,
        distant_values,
        distant_valid,
    )
    attn_low = attended_rows.reshape(row_number, embedding_width).astype(jnp.bfloat16)
    after_attn = inputs + jnp.dot(attn_low, out_weight, preferred_element_type=jnp.float32)
    norm_two, pull_two = jax.vjp(layer_norm, after_attn, norm2_gain, norm2_bias)
    normed_two = norm_two.astype(jnp.bfloat16)
    up_cols = jnp.dot(normed_two, up_weight, preferred_element_type=jnp.float32)
    activated, pull_gelu = jax.vjp(exact_gelu, up_cols)
    hidden = activated.astype(jnp.bfloat16)
    result = after_attn + jnp.dot(hidden, down_weight, preferred_element_type=jnp.float32)
    mixed_out = jnp.where(row_validity[:, None], result, 0.0).astype(jnp.bfloat16)[None]
    grad_out = jnp.where(row_validity[:, None], cotangent[0], jnp.zeros_like(cotangent[0]))
    down_grad = jnp.einsum("tf,td->fd", hidden, grad_out, preferred_element_type=jnp.float32)
    hidden_grad = jnp.einsum("td,fd->tf", grad_out, down_weight, preferred_element_type=jnp.float32)
    (up_slope,) = pull_gelu(hidden_grad)
    up_low = up_slope.astype(jnp.bfloat16)
    up_grad = jnp.einsum("td,tf->df", normed_two, up_low, preferred_element_type=jnp.float32)
    norm_two_in = jnp.einsum("tf,df->td", up_low, up_weight, preferred_element_type=jnp.float32)
    after_part, gain_two_grad, shift_two_grad = pull_two(norm_two_in)
    resid_grad = grad_out.astype(jnp.float32) + after_part
    resid_low = resid_grad.astype(jnp.bfloat16)
    out_grad = jnp.einsum("td,te->de", attn_low, resid_low, preferred_element_type=jnp.float32)
    attn_grad = jnp.einsum("te,de->td", resid_low, out_weight, preferred_element_type=jnp.float32)
    attn_grad = attn_grad.astype(jnp.bfloat16).reshape(row_number, HEADS, HEAD_WIDTH)
    query_gradient, key_grad, value_grad, far_key_grad, far_value_grad = block_backward(
        query_rows,
        key_matrix,
        value_matrix,
        row_validity,
        distant_keys,
        distant_values,
        distant_valid,
        attn_grad,
        row_maximum,
        row_sum_total,
    )
    key_list = [key_grad]
    value_list = [value_grad]
    owned_keys, owned_values = (
        lax.psum_scatter(
            far_key_grad.reshape(distant_count, embedding_width),
            "seq",
            scatter_dimension=0,
            tiled=True,
        ),
        lax.psum_scatter(
            far_value_grad.reshape(distant_count, embedding_width),
            "seq",
            scatter_dimension=0,
            tiled=True,
        ),
    )
    chosen_count = row_number // DILATION_STEP
    segment_count = row_number // SEG
    nearby_keys = jnp.sum(
        jnp.stack(key_list).reshape(segment_count, per_segment, SEG, embedding_width), axis=1
    )
    nearby_values = jnp.sum(
        jnp.stack(value_list).reshape(segment_count, per_segment, SEG, embedding_width), axis=1
    )
    key_total = (
        nearby_keys.reshape(chosen_count, DILATION_STEP, embedding_width)
        .at[:, 0]
        .add(owned_keys)
        .reshape(row_number, embedding_width)
    )
    value_total = (
        nearby_values.reshape(chosen_count, DILATION_STEP, embedding_width)
        .at[:, 0]
        .add(owned_values)
        .reshape(row_number, embedding_width)
    )
    query_total = query_gradient.reshape(row_number, embedding_width)
    mixed_grad = jnp.concatenate(
        [
            (query_total * query_scale).astype(jnp.bfloat16),
            key_total.astype(jnp.bfloat16),
            value_total.astype(jnp.bfloat16),
        ],
        axis=1,
    )
    qkv_grad = jnp.einsum("td,tf->df", normed, mixed_grad, preferred_element_type=jnp.float32)
    norm_one_in = jnp.einsum(
        "tf,df->td", mixed_grad, qkv_weight, preferred_element_type=jnp.float32
    )
    input_part, gain_one_grad, shift_one_grad = pull_one(norm_one_in)
    tokens_grad = (resid_grad + input_part).astype(jnp.bfloat16)[None]
    weight_grads = (qkv_grad, out_grad, up_grad, down_grad)
    row_parts = (
        lax.psum_scatter(weight_grads[0], "seq", scatter_dimension=0, tiled=True),
        lax.psum_scatter(weight_grads[1], "seq", scatter_dimension=0, tiled=True),
        lax.psum_scatter(weight_grads[2], "seq", scatter_dimension=0, tiled=True),
        lax.psum_scatter(weight_grads[3], "seq", scatter_dimension=0, tiled=True),
    )
    final_grads = (
        lax.psum(row_parts[0].astype(jnp.bfloat16), "slide").astype(jnp.float32),
        lax.psum(row_parts[1].astype(jnp.bfloat16), "slide").astype(jnp.float32),
        lax.psum(row_parts[2].astype(jnp.bfloat16), "slide").astype(jnp.float32),
        lax.psum(row_parts[3].astype(jnp.bfloat16), "slide").astype(jnp.float32),
    )
    norm_grads = lax.psum(
        (gain_one_grad, shift_one_grad, gain_two_grad, shift_two_grad), ("seq", "slide")
    )
    return (
        mixed_out,
        tokens_grad,
        final_grads[0],
        final_grads[1],
        final_grads[2],
        final_grads[3],
        norm_grads[0],
        norm_grads[1],
        norm_grads[2],
        norm_grads[3],
    )


MESH = pl.DeviceIdType.MESH
LOW = jnp.bfloat16
FULL = jnp.float32
AUG = 64
LANES = 128
NEVER = -1000000000.0
ANY = pl.BlockSpec(memory_space=pl.ANY)
VMEM = pl.BlockSpec(memory_space=pltpu.VMEM)
SMEM = pl.BlockSpec(memory_space=pltpu.SMEM)


def nn(left, right):
    return jnp.dot(left, right, preferred_element_type=FULL)


def nt(left, right):
    return lax.dot_general(left, right, (((1,), (1,)), ((), ())), preferred_element_type=FULL)


def tn(left, right):
    return lax.dot_general(left, right, (((0,), (0,)), ((), ())), preferred_element_type=FULL)


def remote(src, dst, send_sem, recv_sem, device):
    return pltpu.make_async_remote_copy(
        src_ref=src,
        dst_ref=dst,
        send_sem=send_sem,
        recv_sem=recv_sem,
        device_id=device,
        device_id_type=MESH,
    )


def greet(devices):
    barrier = pltpu.get_barrier_semaphore()
    for device in devices:
        pl.semaphore_signal(barrier, inc=1, device_id=device, device_id_type=MESH)
    pl.semaphore_wait(barrier, len(devices))


def row_peers(count):
    seq, slide = lax.axis_index("seq"), lax.axis_index("slide")
    return [(lax.rem(seq + step, count), slide) for step in range(1, count)]


def spread(ref, values):
    for group in range(ref.shape[0]):
        ref[group] = values[:, group * LANES : (group + 1) * LANES]


def strided_rows(ref, step, count):
    groups = [
        ref[group, pl.ds(step, count, stride=DILATION_STEP), :] for group in range(ref.shape[0])
    ]
    return jnp.concatenate(groups, axis=1)


def strided_store(ref, step, count, values):
    for group in range(ref.shape[0]):
        ref[group, pl.ds(step, count, stride=DILATION_STEP), :] = values[
            :, group * LANES : (group + 1) * LANES
        ]


def chunk(step, size):
    return pl.ds(pl.multiple_of(step * size, size), size)


def steps(body):
    @pl.loop(0, DILATION_STEP // 4)
    def _(group):
        for member in range(4):
            body(group * 4 + member)


def row_mean(values):
    return jnp.mean(values, axis=-1, keepdims=True)


def fold_rows(values):
    return jnp.sum(values.reshape(-1, 8, values.shape[-1]), axis=0)


def mask_rows(ref, bias):
    first = lax.broadcasted_iota(jnp.int32, (AUG - HEAD_WIDTH, ref.shape[2]), 0) == 0
    ref[:, HEAD_WIDTH:, :] = jnp.broadcast_to(
        jnp.where(first, bias, 0.0).astype(LOW), (HEADS, AUG - HEAD_WIDTH, ref.shape[2])
    )


class Place:
    def __init__(self):
        seq, slide = lax.axis_index("seq"), lax.axis_index("slide")
        self.seq, self.slide = seq, slide
        self.z, self.x = seq // 2, seq % 2
        self.b, self.a = self.z // 2, self.z % 2
        self.y, self.c = slide // 2, slide % 2
        self.sibling = (seq, slide + 1 - 2 * self.c)
        self.across_y = (seq, slide + 2 - 4 * self.y)
        self.diagonal = (seq, 3 - slide)
        self.across_x = (seq + 1 - 2 * self.x, slide)
        self.slide_peers = (self.sibling, self.across_y, self.diagonal)

    def layer(self, step):
        return (self.z + step) % 4


class Part:
    def __init__(self, place, orders, both, core_got, got, final, send_sem, recv_sem):
        self.place, self.orders, self.both = place, orders, both
        self.core_got, self.got, self.final = core_got, got, final
        self.send_sem, self.recv_sem = send_sem, recv_sem
        self.folds = max(len(order) for order in orders)

    def blocks(self, core, phase, value):
        choices = {}
        for at, name in enumerate(self.orders[core], 1):
            if at < phase:
                choices[name] = [getattr(self.place, name)]
            elif at == phase:
                choices[name] = [value]
            else:
                choices[name] = list(range(4 if name == "z" else 2))
        if "z" not in choices:
            choices["z"] = [2 * b + a for b in choices["b"] for a in choices["a"]]
        return [(2 * z + x, y) for z in choices["z"] for x in choices["x"] for y in choices["y"]]

    def partners(self, core, phase):
        place, name = self.place, self.orders[core][phase - 1]
        if name == "x":
            return [(1 - place.x, place.across_x)]
        if name == "y":
            return [(1 - place.y, place.across_y)]
        if name == "a":
            return [(1 - place.a, (place.seq + 2 - 4 * place.a, place.slide))]
        if name == "b":
            return [(1 - place.b, (place.seq + 4 - 8 * place.b, place.slide))]
        layers = [place.layer(k) for k in (1, 2, 3)]
        return [(z, (2 * z + place.x, place.slide)) for z in layers]

    def span(self, core, phase):
        first, left = 0, 16
        for at, name in enumerate(self.orders[core], 1):
            left //= 4 if name == "z" else 2
            number = left * (3 if name == "z" else 1)
            if at == phase:
                return first, number
            first += number

    def transfers(self, core, phase):
        kept, got = self.both.at[0], self.got
        slot = self.span(core, phase)[0]
        pairs = "y" in self.orders[core][phase:]
        moves = []
        for value, device in self.partners(core, phase):
            for owner, y in self.blocks(core, phase, value):
                if not pairs:
                    moves.append((kept.at[owner, y], got.at[slot], device))
                elif y == 0:
                    moves.append((kept.at[owner], got.at[pl.ds(slot, 2)], device))
                slot += 1
        return moves

    def start(self, phase, merged):
        place, send, recv = self.place, self.send_sem.at[phase], self.recv_sem.at[phase]
        if phase == 0:
            remote(self.both.at[1], self.core_got, send, recv, place.sibling).start()
        elif phase <= self.folds:
            for core in range(2):
                if phase > len(self.orders[core]):
                    continue

                @pl.when(place.c == core)
                def _(core=core):
                    for source, target, device in self.transfers(core, phase):
                        remote(source, target, send, recv, device).start()
        elif phase == self.folds + 1:
            own = self.final.at[place.c * 2 + place.y]
            for device in place.slide_peers if merged else (place.across_y,):
                remote(own, own, send, recv, device).start()
        else:
            own = self.final.at[pl.ds(place.c * 2, 2)]
            remote(own, own, send, recv, place.sibling).start()

    def wait(self, phase, whole):
        both_ways = remote(
            whole, whole, self.send_sem.at[phase], self.recv_sem.at[phase], self.place.sibling
        )
        both_ways.wait_recv()
        both_ways.wait_send()

    def finish(self, phase, merged):
        place = self.place
        if phase == 0:
            self.wait(phase, self.core_got)

            @pl.loop(0, 8)
            def _(owner):
                for row in range(2):
                    self.both[0, owner, row] += self.core_got[owner, row]
        elif phase <= self.folds:
            for core in range(2):
                if phase > len(self.orders[core]):
                    continue

                @pl.when(place.c == core)
                def _(core=core):
                    first, number = self.span(core, phase)
                    self.wait(phase, self.got.at[pl.ds(first, number)])
                    name = self.orders[core][phase - 1]
                    blocks = self.blocks(core, phase, getattr(place, name))
                    for n, (owner, y) in enumerate(blocks):
                        slots = range(first + n, first + number, len(blocks))
                        self.add(owner, y, slots, core if phase == len(self.orders[core]) else None)
        elif phase == self.folds + 1:
            self.wait(phase, self.final.at[pl.ds(0, 3 if merged else 1)])
        else:
            self.wait(phase, self.final.at[pl.ds(0, 2)])

    def add(self, owner, y, slots, core):
        if len(slots) == 1:
            total = self.both[0, owner, y] + self.got[slots[0]]
        else:
            total = self.both[0, owner, y].astype(FULL)
            for slot in slots:
                total = total + self.got[slot].astype(FULL)
            total = total.astype(LOW)
        if core is None:
            self.both[0, owner, y] = total
        else:
            self.final[core * 2 + self.place.y] = total


class Piece:
    def __init__(self, parts, merged, outs, out_sem):
        self.parts, self.merged, self.outs, self.out_sem = parts, merged, outs, out_sem
        self.last = parts[0].folds + (1 if merged else 2)
        self.phase = -1

    @property
    def done(self):
        return self.phase > self.last

    def advance(self):
        if self.done:
            return
        if self.phase >= 0:
            for part in self.parts:
                part.finish(self.phase, self.merged)
        self.phase += 1
        if not self.done:
            for part in self.parts:
                part.start(self.phase, self.merged)
            return
        for n in range(len(self.parts)):
            self.out_copy(n).start()

    def out_copy(self, n):
        return pltpu.make_async_copy(self.parts[n].final, self.outs[n], self.out_sem.at[n])


TILES = 3
LASTS = 4
PIECES = TILES + LASTS
ORDERS = (
    ("abxy", "yxz", False),
    ("yxab", "xzy", False),
    ("yxz", "yaxb", False),
    ("yxab", "xyab", True),
    ("yxab", "xyab", True),
    ("yxab", "xyab", True),
    ("yxab", "ayxb", True),
)
HOOKS = {
    "tile1.1": (0,),
    "tile2.1": (1,),
    "after0": (0,),
    "after1": (2,),
    "far": (1,),
    "near0": (0,),
    "near4": (3,),
    "near5": (4,),
    "near6": (2,),
    "last2": (3,),
    "last3": (1, 5),
    "into": (6, 4, 0, 2),
    "norm": (1,),
}
TAIL = (3, 5, 4, 6, 2, 0, 1, 5, 3, 6, 4, 2, 5, 0, 3, 1, 6, 4, 1, 0, 5, 2, 3, 6, 4, 2, 5, 6)

def main_kernel(
    count, tokens, cotangent, qkv_weight, out_weight, up_weight, down_weight,
    gain_one, shift_one, gain_two, shift_two, visible,
    mixed_out, tokens_out, down_sums, up_sums, last_sums, norm_out, weights_kept, norm_kept,
    normed, far_normed, query, key, value, far_key, far_value, far_weights, scale, far_scale, attn,
    delta, slope, resid, after, dyb, wqkv, wo, wide, staged, all_far, far_got, spread_one,
    sums, around, across,
    down_both, up_both, last_both, down_core, up_core, last_core,
    down_got, up_got, last_got, down_final, up_final, last_final,
    load_sem, tile_sem, group_sem, store_sem, out_sem, send_sem, recv_sem,
    gather_send_sem, gather_recv_sem, far_send_sem, far_recv_sem, norm_send_sem, norm_recv_sem,
):
    place = Place()
    seq, core = place.seq, place.c
    rows, width = resid.shape
    chosen = rows // DILATION_STEP
    group_lanes = LANES
    tile_width = count * group_lanes
    first_row = seq * rows
    limit = visible[0]
    peers = row_peers(count)
    others = list(place.slide_peers) + peers
    barrier = pltpu.get_barrier_semaphore()
    for other in others:
        pl.semaphore_signal(barrier, inc=1, device_id=other, device_id_type=MESH)

    def valid_rows(step):
        places = lax.broadcasted_iota(jnp.int32, (chosen, 1), 0) * DILATION_STEP + step
        return first_row + places < limit

    def landed(n):
        sources = (
            (tokens, staged),
            (qkv_weight.at[:, pl.ds(width, width)], wqkv.at[1]),
            (qkv_weight.at[:, pl.ds(2 * width, width)], wqkv.at[2]),
            (qkv_weight.at[:, pl.ds(0, width)], wqkv.at[0]),
            (out_weight, wo),
            (cotangent, staged),
        )
        return pltpu.make_async_copy(*sources[n], load_sem.at[n])

    for n in range(5):
        landed(n).start()
    distant = count * chosen
    members = 4

    def kept_group(group, slots):
        kept = weights_kept.at[pl.ds(group * members, members)]
        return slots.at[group % 2], kept, group_sem.at[group % 2]

    pieces = []
    for n in range(TILES):
        parts = [
            Part(
                place,
                ORDERS[n][:2],
                both.at[n],
                core_got.at[n],
                got.at[n],
                final.at[n],
                send_sem.at[n, which],
                recv_sem.at[n, which],
            )
            for which, (both, core_got, got, final) in enumerate(
                (
                    (down_both, down_core, down_got, down_final),
                    (up_both, up_core, up_got, up_final),
                )
            )
        ]
        pieces.append(Piece(parts, ORDERS[n][2], (down_sums.at[n], up_sums.at[n]), out_sem.at[n]))
    for n in range(LASTS):
        part = Part(
            place,
            ORDERS[TILES + n][:2],
            last_both.at[n],
            last_core.at[n],
            last_got.at[n],
            last_final.at[n],
            send_sem.at[TILES + n, 0],
            recv_sem.at[TILES + n, 0],
        )
        pieces.append(Piece([part], ORDERS[TILES + n][2], (last_sums.at[n],), out_sem.at[TILES + n]))

    def hook(name):
        for n in HOOKS.get(name, ()):
            if pieces[n].phase >= 0:
                pieces[n].advance()

    def split_last(n, side, grads):
        target = last_both.at[n, (side + core) % 2]
        target[...] = grads.astype(LOW).reshape(count, 2, -1, grads.shape[1])

    def attend_part(h1, top, total, attended, weights):
        landed(0).wait()
        spread(wide, staged[...].astype(FULL))
        landed(5).start()

        def normalize(step):
            at = chunk(step, chosen)
            values = strided_rows(wide, step, chosen)
            centered = values - row_mean(values)
            inverse = lax.rsqrt(row_mean(centered * centered) + epsilon)
            normal = centered * inverse
            after[at] = values
            resid[at] = normal
            spread_one[at] = jnp.broadcast_to(inverse, (chosen, LANES))
            low = (normal * gain_one[...][None] + shift_one[...][None]).astype(LOW)
            h1[at] = low
            return low

        all_far[seq] = normalize(0)

        @pl.loop(0, 5)
        def _(group):
            for member in range(3):
                normalize(group * 3 + member + 1)

        pltpu.make_async_copy(resid, norm_kept, store_sem.at[0]).start()
        for part, ref in ((1, key), (2, value)):
            landed(part).wait()
            projected = nn(h1[...], wqkv[part]).astype(LOW)
            ref[:, :HEAD_WIDTH, :] = projected.T.reshape(HEADS, HEAD_WIDTH, rows)
            if part == 1:
                pl.semaphore_wait(barrier, len(others))
                for n, peer in enumerate(peers):
                    mine = all_far.at[seq]
                    send, recv = gather_send_sem.at[n], gather_recv_sem.at[n]
                    remote(mine, mine, send, recv, peer).start()
        landed(3).wait()
        projected = (nn(h1[...], wqkv[0]) * HEAD_WIDTH ** (-0.5)).astype(LOW)
        query[:, :HEAD_WIDTH, :] = projected.T.reshape(HEADS, HEAD_WIDTH, rows)
        places = lax.broadcasted_iota(jnp.int32, (1, rows), 1)
        places = first_row + (places % chosen) * DILATION_STEP + places // chosen
        mask_rows(key, jnp.where(places < limit, 0.0, NEVER))
        mask_rows(query, jnp.ones((1, rows), FULL))

        @pl.loop(0, HEADS // members)
        def _(group):
            slot, kept, sem = kept_group(group, weights)

            @pl.when(group >= 2)
            def _():
                pltpu.make_async_copy(slot, kept, sem).wait()

            for member in range(members):
                head = group * members + member
                scores = tn(key[head], query[head])
                highest = jnp.max(scores, axis=0, keepdims=True)
                exponent = jnp.exp(scores - highest)
                top[head] = highest
                total[head] = jnp.sum(exponent, axis=0, keepdims=True)
                low = exponent.astype(LOW)
                weights[group % 2, member] = low
                attended[head] = nn(value[head], low)
            pltpu.make_async_copy(slot, kept, sem).start()

        normed[...] = h1[...].T
        landed(5).wait()
        spread(wide, staged[...].astype(FULL))

        @steps
        def _(step):
            at = chunk(step, chosen)
            dyb[at] = jnp.where(valid_rows(step), strided_rows(wide, step, chosen), 0.0).astype(LOW)

        for n in range(count - 1):
            source = lax.rem(seq + count - 1 - n, count)
            mine, theirs = all_far.at[seq], all_far.at[source]
            wait = remote(mine, theirs, gather_send_sem.at[n], gather_recv_sem.at[n], peers[0])
            wait.wait_recv()
            wait.wait_send()
        flat = all_far[...].reshape(distant, width)
        for part, ref in ((1, far_key), (2, far_value)):
            projected = nn(flat, wqkv[part]).astype(LOW)
            ref[:, :HEAD_WIDTH, :] = projected.T.reshape(HEADS, HEAD_WIDTH, distant)
        places = lax.broadcasted_iota(jnp.int32, (1, distant), 1) * DILATION_STEP
        mask_rows(far_key, jnp.where(places < limit, 0.0, NEVER))
        lane_mask = jnp.where(lax.broadcasted_iota(jnp.int32, (1, LANES), 1) < chosen, 0.0, NEVER)

        @pl.loop(0, HEADS // 4)
        def _(group):
            for member in range(4):
                head = group * 4 + member
                scores = tn(far_key[head], query[head][:, :LANES]) + lane_mask
                highest = jnp.max(scores, axis=0, keepdims=True)
                exponent = jnp.exp(scores - highest)
                low = exponent.astype(LOW)
                far_weights[head] = low
                near = top[head][:, :LANES]
                joint = jnp.maximum(near, highest)
                near_part, far_part = jnp.exp(near - joint), jnp.exp(highest - joint)
                joint_total = total[head][:, :LANES] * near_part + far_part * jnp.sum(
                    exponent, axis=0, keepdims=True
                )
                near_part, far_part = near_part / joint_total, far_part / joint_total
                far_scale[head] = far_part
                local = jnp.concatenate([near_part, 1.0 / total[head][:, LANES:]], axis=1)
                scale[head] = local
                result = attended[head] * local
                with_far = result[:, :LANES] + nn(far_value[head], low) * far_part
                result = jnp.concatenate([with_far, result[:, LANES:]], axis=1)
                attn[head] = result.astype(LOW)

        for group in (2, 3):
            slot, kept, sem = kept_group(group, weights)
            pltpu.make_async_copy(slot, kept, sem).wait()
        pltpu.make_async_copy(resid, norm_kept, store_sem.at[0]).wait()

    vm = pltpu.VMEM
    pl.run_scoped(
        attend_part,
        vm((rows, width), LOW),
        vm((HEADS, 1, rows), FULL),
        vm((HEADS, 1, rows), FULL),
        vm((HEADS, HEAD_WIDTH, rows), FULL),
        vm((2, members, rows, rows), LOW),
    )

    def forward_part(norm_two, spread_two, h2, h2_t, active, low_slope, wup, wdown):
        halves = 2
        per_half = tile_width // halves

        def load_tile(tile, half):
            for local in range(count // halves):
                owner = half * (count // halves) + local
                first = owner * TILES * group_lanes + tile * group_lanes
                at = pl.ds(pl.multiple_of(first, LANES), group_lanes)
                to = pl.ds(local * group_lanes, group_lanes)
                pltpu.make_async_copy(
                    up_weight.at[:, at], wup.at[half, :, to], tile_sem.at[half, 0]
                ).start()
                pltpu.make_async_copy(
                    down_weight.at[at], wdown.at[half, to], tile_sem.at[half, 1]
                ).start()

        def wait_tile(half):
            pltpu.make_async_copy(wup.at[half], wup.at[half], tile_sem.at[half, 0]).wait()
            pltpu.make_async_copy(wdown.at[half], wdown.at[half], tile_sem.at[half, 1]).wait()

        load_tile(0, 0)
        load_tile(0, 1)
        landed(4).wait()
        after[...] += nn(attn[...].reshape(width, rows).T, wo[...])

        @steps
        def _(step):
            at = chunk(step, chosen)
            values = after[at]
            centered = values - row_mean(values)
            inverse = lax.rsqrt(row_mean(centered * centered) + epsilon)
            normal = centered * inverse
            norm_two[at] = normal
            spread_two[at] = jnp.broadcast_to(inverse, (chosen, LANES))
            h2[at] = (normal * gain_two[...][None] + shift_two[...][None]).astype(LOW)
            resid[at] = jnp.zeros((chosen, width), FULL)

        h2_t[...] = h2[...].T
        for tile in range(TILES):
            @pl.loop(0, halves)
            def _(half, tile=tile):
                wait_tile(half)
                for part in range(2):
                    at = slice(part * per_half // 2, (part + 1) * per_half // 2)
                    to = pl.ds(
                        pl.multiple_of(half * per_half + part * per_half // 2, LANES), per_half // 2
                    )
                    hidden = nn(h2[...], wup[half, :, at])
                    hidden_slope = nt(dyb[...], wdown[half, at])
                    share = 0.5 * (1.0 + lax.erf(hidden * 0.7071067811865476))
                    active[:, to] = (hidden * share).astype(LOW)
                    density = hidden * jnp.exp(-0.5 * hidden * hidden) * 0.3989422804014327
                    low_slope[:, to] = (hidden_slope * (share + density)).astype(LOW)
                to = pl.ds(pl.multiple_of(half * per_half, LANES), per_half)
                after[...] += nn(active[:, to], wdown[half])
                resid[...] += nt(low_slope[:, to], wup[half])
                if tile + 1 < TILES:
                    load_tile(tile + 1, half)

            hook("tile%d.1" % tile)

            @pl.loop(0, 4)
            def _(part, tile=tile):
                at = pl.ds(pl.multiple_of(part * tile_width // 4, LANES), tile_width // 4)
                grads = nn(h2_t[...], low_slope[:, at]).astype(LOW)
                target = up_both.at[tile, (part // 2 + core) % 2]
                target[:, part % 2] = grads.reshape(count, -1, grads.shape[1])
                grads = tn(active[:, at], dyb[...]).astype(LOW)
                owners = count // 4
                grads = grads.reshape(owners, 2, 2, -1, width)
                for side in range(2):
                    target = down_both.at[tile, (side + core) % 2]
                    target[pl.ds(part * owners, owners)] = grads[:, side]

            pieces[tile].advance()
            hook("tile%d.3" % tile)
        sums[...] = jnp.zeros_like(sums)
        hook("after0")

        @steps
        def _(step):
            at = chunk(step, chosen)
            strided_store(wide, step, chosen, jnp.where(valid_rows(step), after[at], 0.0))
            given, normal = resid[at], norm_two[at]
            sums[2] += fold_rows(given * normal)
            sums[3] += fold_rows(given)
            scaled = given * gain_two[...][None]
            part = scaled - row_mean(scaled) - normal * row_mean(scaled * normal)
            value_here = dyb[at].astype(FULL) + spread_two[at][:, :1] * part
            resid[at] = value_here
            h2[at] = value_here.astype(LOW)

        for group in range(width // LANES):
            staged[:, group * LANES : (group + 1) * LANES] = wide[group].astype(LOW)
        pltpu.make_async_copy(staged, mixed_out, store_sem.at[1]).start()
        half = width // 2
        hook("after1")
        for n in range(2):
            at = slice(n * half, (n + 1) * half)
            split_last(2 * n + 1, 1, nn(attn[...].reshape(width, rows), h2[:, at]))
        slope[...] = nt(wo[...], h2[...]).astype(LOW).reshape(HEADS, HEAD_WIDTH, rows)

        @pl.loop(0, HEADS)
        def _(head):
            product = slope[head].astype(FULL) * attn[head].astype(FULL)
            delta[head] = jnp.sum(product, axis=0, keepdims=True)

        hook("after2")

    pl.run_scoped(
        forward_part,
        vm((rows, width), FULL),
        vm((rows, LANES), FULL),
        vm((rows, width), LOW),
        vm((width, rows), LOW),
        vm((rows, tile_width), LOW),
        vm((rows, tile_width), LOW),
        vm((2, width, tile_width // 2), LOW),
        vm((2, tile_width // 2, width), LOW),
    )

    def backward_part(weights, slopes, far_query, far_send, given):
        norm_one = after

        def load_group(group):
            slot, kept, sem = kept_group(group, weights)
            return pltpu.make_async_copy(kept, slot, sem)

        load_group(0).start()
        load_group(1).start()
        norm_load = pltpu.make_async_copy(norm_kept, norm_one, store_sem.at[0])
        norm_load.start()

        @pl.loop(0, HEADS // 4)
        def _(group):
            for member in range(4):
                head = group * 4 + member
                first_slope = slope[head][:, :LANES]
                low = far_weights[head]
                change = tn(far_value[head], first_slope) - delta[head][:, :LANES]
                score_slope = (low.astype(FULL) * far_scale[head] * change).astype(LOW)
                far_query[head] = nn(far_key[head, :HEAD_WIDTH], score_slope)
                scaled = (first_slope.astype(FULL) * far_scale[head]).astype(LOW)
                given[0, head] = nt(query[head, :HEAD_WIDTH, :LANES], score_slope).astype(LOW)
                given[1, head] = nt(scaled, low).astype(LOW)

        hook("far0")
        far_normed[...] = all_far[...].reshape(distant, width).T
        into = nn(wqkv[1], given[0].reshape(width, distant))
        into += nn(wqkv[2], given[1].reshape(width, distant))
        far_send[...] = into.T.astype(LOW).reshape(count, chosen, width)
        for n, peer in enumerate(peers):
            remote(
                far_send.at[peer[0]], far_got.at[n], far_send_sem.at[n], far_recv_sem.at[n], peer
            ).start()
        hook("far")

        def weight_slopes(half):
            at = slice(half * HEADS // 2, (half + 1) * HEADS // 2)
            for part, (n, side) in enumerate(((0, 0), (0, 1), (1, 0))):
                grads = nt(normed[...], slopes[part, at].reshape(width // 2, rows))
                if part:
                    far = given[part - 1, at].reshape(width // 2, distant)
                    grads += nt(far_normed[...], far)
                split_last(2 * half + n, side, grads)
                if part:
                    pieces[TILES + 2 * half + n].advance()
                    hook("last%d" % (2 * half + n))

        for group in range(HEADS // members):
            load_group(group).wait()
            for member in range(members):
                head = group * members + member
                low = weights[group % 2, member]
                change = tn(value[head], slope[head]) - delta[head]
                score_slope = (low.astype(FULL) * scale[head] * change).astype(LOW)
                query_slope = nn(key[head, :HEAD_WIDTH], score_slope)
                key_slope = nt(query[head, :HEAD_WIDTH], score_slope)
                scaled = (slope[head].astype(FULL) * scale[head]).astype(LOW)
                value_slope = nt(scaled, low)
                first = query_slope[:, :LANES] + far_query[head]
                query_slope = jnp.concatenate([first, query_slope[:, LANES:]], axis=1)
                slopes[0, head] = (query_slope * HEAD_WIDTH ** (-0.5)).astype(LOW)
                slopes[1, head] = key_slope.astype(LOW)
                slopes[2, head] = value_slope.astype(LOW)
                if member % 2:
                    hook("near%d" % (head // 2))
            if (group + 2) * members < HEADS:
                load_group(group + 2).start()
            if group % 2:
                weight_slopes(group // 2)

        def flat_slopes(part):
            return slopes[part].reshape(width, rows)

        into = nn(wqkv[0], flat_slopes(0))
        into += nn(wqkv[1], flat_slopes(1))
        into += nn(wqkv[2], flat_slopes(2))
        norm_load.wait()
        pltpu.make_async_copy(staged, mixed_out, store_sem.at[1]).wait()
        spread(wide, into.T)
        hook("into")
        total = far_send[seq].astype(FULL)
        for n in range(count - 1):
            wait = remote(
                far_got.at[n], far_got.at[n], far_send_sem.at[n], far_recv_sem.at[n], peers[0]
            )
            wait.wait_recv()
            wait.wait_send()
            total = total + far_got[n].astype(FULL)
        for group in range(width // LANES):
            wide[group, :chosen] += total[:, group * LANES : (group + 1) * LANES]

        @steps
        def _(step):
            at = chunk(step, chosen)
            here = jnp.concatenate([wide[group, at, :] for group in range(width // LANES)], axis=1)
            normal = norm_one[at]
            sums[0] += fold_rows(here * normal)
            sums[1] += fold_rows(here)
            scaled = here * gain_one[...][None]
            part = scaled - row_mean(scaled) - normal * row_mean(scaled * normal)
            resid[at] += spread_one[at][:, :1] * part

    pl.run_scoped(
        backward_part,
        vm((2, members, rows, rows), LOW),
        vm((3, HEADS, HEAD_WIDTH, rows), LOW),
        vm((HEADS, HEAD_WIDTH, LANES), FULL),
        vm((count, chosen, width), LOW),
        vm((2, HEADS, HEAD_WIDTH, distant), LOW),
    )
    for n in range(4):
        around[seq, pl.ds(n, 1)] = jnp.sum(sums[n], axis=0, keepdims=True)
    for n, peer in enumerate(peers):
        mine = around.at[seq]
        remote(mine, mine, norm_send_sem.at[n], norm_recv_sem.at[n], peer).start()
    hook("norm")

    @steps
    def _(step):
        strided_store(wide, step, chosen, resid[chunk(step, chosen)])

    for group in range(width // LANES):
        staged[:, group * LANES : (group + 1) * LANES] = wide[group].astype(LOW)
    tokens_copy = pltpu.make_async_copy(staged, tokens_out, store_sem.at[2])
    tokens_copy.start()
    for n in range(count - 1):
        mine = around.at[seq]
        wait = remote(mine, mine, norm_send_sem.at[n], norm_recv_sem.at[n], peers[0])
        wait.wait_recv()
        wait.wait_send()
    total = around[0]
    for n in range(1, count):
        total = total + around[n]
    across[place.slide] = total
    for n, peer in enumerate(place.slide_peers):
        mine, at = across.at[place.slide], count - 1 + n
        remote(mine, mine, norm_send_sem.at[at], norm_recv_sem.at[at], peer).start()
    for n in TAIL + tuple(range(PIECES)) * 6:
        pieces[n].advance()
    for n in range(3):
        mine, at = across.at[0], count - 1 + n
        wait = remote(mine, mine, norm_send_sem.at[at], norm_recv_sem.at[at], peers[0])
        wait.wait_recv()
        wait.wait_send()
    norm_out[...] = (across[0] + across[1]) + (across[2] + across[3])
    for piece in pieces:
        for n in range(len(piece.parts)):
            piece.out_copy(n).wait()
    tokens_copy.wait()


def main_pass(count, tokens, cotangent, weights, norms, visible):
    rows, width = tokens.shape
    chosen = rows // DILATION_STEP
    distant = count * chosen
    owned = width // count
    vm, dma = pltpu.VMEM, pltpu.SemaphoreType.DMA
    down_block, up_block = (LANES // 4, width), (owned, 2 * LANES)
    last_block = (owned // 2, width // 2)
    blocks = ((TILES, down_block), (TILES, up_block), (LASTS, last_block))
    low = [
        (width, rows), (width, distant), (HEADS, AUG, rows), (HEADS, AUG, rows),
        (HEADS, HEAD_WIDTH, rows), (HEADS, AUG, distant), (HEADS, HEAD_WIDTH, distant),
        (HEADS, distant, LANES),
    ]
    scratch = [vm(shape, LOW) for shape in low]
    scratch += [
        vm((HEADS, 1, rows), FULL),
        vm((HEADS, 1, LANES), FULL),
        vm((HEADS, HEAD_WIDTH, rows), LOW),
        vm((HEADS, 1, rows), FULL),
        vm((HEADS, HEAD_WIDTH, rows), LOW),
        vm((rows, width), FULL),
        vm((rows, width), FULL),
        vm((rows, width), LOW),
        vm((3, width, width), LOW),
        vm((width, width), LOW),
        vm((width // LANES, rows, LANES), FULL),
        vm((rows, width), LOW),
        vm((count, chosen, width), LOW),
        vm((count - 1, chosen, width), LOW),
        vm((rows, LANES), FULL),
        vm((4, 8, width), FULL),
        vm((count, 8, width), FULL),
        vm((4, 8, width), FULL),
    ]
    scratch += [vm((n, 2, count, 2) + block, LOW) for n, block in blocks]
    scratch += [vm((n, count, 2) + block, LOW) for n, block in blocks]
    scratch += [vm((n, 15) + block, LOW) for n, block in blocks]
    scratch += [vm((n, 4) + block, LOW) for n, block in blocks]
    scratch += [
        dma((6,)), dma((2, 2)), dma((2,)), dma((3,)), dma((PIECES, 2)),
        dma((PIECES, 2, 7)), dma((PIECES, 2, 7)),
        dma((count - 1,)), dma((count - 1,)), dma((count - 1,)), dma((count - 1,)),
        dma((count + 2,)), dma((count + 2,)),
    ]
    sums = [jax.ShapeDtypeStruct((n, 4) + block, LOW) for n, block in blocks]
    results = pl.pallas_call(
        functools.partial(main_kernel, count),
        out_shape=(
            jax.ShapeDtypeStruct((rows, width), LOW),
            jax.ShapeDtypeStruct((rows, width), LOW),
            *sums,
            jax.ShapeDtypeStruct((8, width), FULL),
            jax.ShapeDtypeStruct((HEADS, rows, rows), LOW),
            jax.ShapeDtypeStruct((rows, width), FULL),
        ),
        in_specs=[ANY] * 6 + [VMEM] * 4 + [SMEM],
        out_specs=(ANY, ANY, ANY, ANY, ANY, VMEM, ANY, ANY),
        scratch_shapes=scratch,
        compiler_params=pltpu.CompilerParams(
            collective_id=1, has_side_effects=True, vmem_limit_bytes=64 << 20
        ),
        name="main_pass",
    )(tokens, cotangent, *weights, *norms, visible)
    return results[:6]


def finish_kernel(
    mixed, tokens_grad, down_sums, up_sums, last_sums, norms,
    mixed_out, tokens_out, qkv_out, out_out, up_out, down_out, *refs
):
    norm_outs = refs[:4]
    mixed_in, tokens_in, down_in, up_in, last_in, norms_in = refs[4:10]
    qkv, out, up, down, in_sem, out_sem = refs[10:]
    loads = [
        pltpu.make_async_copy(source, target, in_sem.at[n])
        for n, (source, target) in enumerate(
            (
                (down_sums, down_in),
                (up_sums, up_in),
                (last_sums, last_in),
                (norms, norms_in),
                (mixed, mixed_in),
                (tokens_grad, tokens_in),
            )
        )
    ]
    for copy in loads:
        copy.start()
    stores = []

    def store(source, target):
        copy = pltpu.make_async_copy(source, target, out_sem.at[len(stores)])
        copy.start()
        stores.append(copy)

    tiles, blocks, rows, _ = down_sums.shape
    loads[0].wait()
    for tile in range(tiles):
        for block in range(blocks):
            first = (tile * blocks + block) * rows
            down[first : first + rows] = down_in[tile, block].astype(FULL)
    store(down, down_out)
    loads[1].wait()
    for tile in range(tiles):
        for block in range(blocks):
            for half in range(2):
                first = ((block * 2 + half) * tiles + tile) * LANES
                part = up_in[tile, block][:, half * LANES : (half + 1) * LANES]
                up[:, first : first + LANES] = part.astype(FULL)
    store(up, up_out)
    loads[2].wait()
    rows, columns = last_sums.shape[2:]
    for piece in range(last_sums.shape[0]):
        half, pair = divmod(piece, 2)
        for block in range(blocks):
            side, row = divmod(block, 2)
            at = slice(row * rows, (row + 1) * rows)
            first = half * columns
            target = out
            if pair == 0 or side == 0:
                target, first = qkv, first + 2 * columns * (2 * pair + side)
            target[at, first : first + columns] = last_in[piece, block].astype(FULL)
    store(qkv, qkv_out)
    store(out, out_out)
    loads[3].wait()
    for n, norm_out in enumerate(norm_outs):
        norm_out[...] = norms_in[n]
    for n, (source, target) in enumerate(((mixed_in, mixed_out), (tokens_in, tokens_out))):
        loads[4 + n].wait()
        store(source, target)
    for copy in stores:
        copy.wait()


def finish_pass(count, results):
    rows, width = results[0].shape
    owned = width // count

    def full(*shape):
        return jax.ShapeDtypeStruct(shape, FULL)

    grads = [
        full(owned, 3 * width),
        full(owned, width),
        full(owned, TILES * count * LANES),
        full(TILES * LANES, width),
    ]
    return pl.pallas_call(
        finish_kernel,
        out_shape=(
            jax.ShapeDtypeStruct((rows, width), LOW),
            jax.ShapeDtypeStruct((rows, width), LOW),
            *grads,
            *[full(width)] * 4,
        ),
        in_specs=[ANY] * 6,
        out_specs=(ANY,) * 6 + (VMEM,) * 4,
        scratch_shapes=[pltpu.VMEM(ref.shape, ref.dtype) for ref in (*results, *grads)]
        + [pltpu.SemaphoreType.DMA((6,)), pltpu.SemaphoreType.DMA((6,))],
        compiler_params=pltpu.CompilerParams(vmem_limit_bytes=63 << 20),
        name="finish_pass",
    )(*results)


def fused_device(
    tokens,
    qkv_weight,
    out_weight,
    up_weight,
    down_weight,
    norm1_gain,
    norm1_bias,
    norm2_gain,
    norm2_bias,
    visible,
    cotangent,
):
    count = lax.axis_size("seq")
    results = main_pass(
        count,
        tokens[0],
        cotangent[0],
        (qkv_weight, out_weight, up_weight, down_weight),
        (norm1_gain, norm1_bias, norm2_gain, norm2_bias),
        visible,
    )
    mixed, tokens_grad, *grads = finish_pass(count, results)
    return (mixed[None], tokens_grad[None], *grads)


def solution(mesh):
    placed = (
        P("slide", "seq", None),
        P(),
        P(),
        P(),
        P(),
        P(),
        P(),
        P(),
        P(),
        P("slide"),
        P("slide", "seq", None),
    )
    fused = mesh.shape["seq"] == 8 and mesh.shape["slide"] == 4
    return jax.shard_map(
        fused_device if fused else plain_device,
        mesh=mesh,
        in_specs=placed,
        out_specs=(
            P("slide", "seq", None),
            P("slide", "seq", None),
            P("seq", None),
            P("seq", None),
            P("seq", None),
            P("seq", None),
            P(),
            P(),
            P(),
            P(),
        ),
        check_vma=False,
    )
```

profile of v0, /device:TPU:0, one launch (start us, length us, event | category | flops | bytes accessed | tf_op | source)
XLA Modules:
  0.0 122.8 jit_solution(11718736718370542518)
XLA Ops:
  1.3 117.2 %main_pass.1 = (bf16[512,768]{1,0:T(8,128)(2,1)}, bf16[512,768]{1,0:T(8,128)(2,1)}, bf16[3,4,32,768]{3,2,1,0:T(8,128)(2,1)}, bf16[3,4,96,256]{3,2,1,0:T(8,128)(2...) custom-call(bf16[512,768]{1,0:T(8,128)(2,1)} %bitcast.4, ...), custom_call_target="tpu_custom_call" | custom-call | tf_op jit(solution)/shard_map/main_pass/pallas_call | solution.py:1153
  118.5 4.1 %finish_pass.1 = (bf16[512,768]{1,0:T(8,128)(2,1)}, bf16[512,768]{1,0:T(8,128)(2,1)}, f32[96,2304]{1,0:T(8,128)}, f32[96,768]{1,0:T(8,128)}, f32[96,3072]{1,0:T(...) custom-call(bf16[512,768]{1,0:T(8,128)(2,1)} %get-tuple-element.26.mixed, ...), custom_call_target="tpu_custom_call" | custom-call | tf_op jit(solution)/shard_map/finish_pass/pallas_call | solution.py:1255
where the time goes:
time: 123 us
  Pallas kernels  121 us (98%)
  between operations  1.48 us (1%)
    pallas_call x1, Pallas kernels, main_pass(): pl.pallas_call(functools.partial(main_kernel, count), out_shape=(jax.Shap...  117 us
    pallas_call x1, Pallas kernels, finish_pass(): pl.pallas_call(finish_kernel, out_shape=(jax.ShapeDtypeStruct((rows, widt...  4.14 us

commit v1 on v0

--- a/solution.py
+++ b/solution.py
@@ -325,7 +325,7 @@
 FULL = jnp.float32
 AUG = 64
 LANES = 128
-NEVER = -1000000000.0
+NEVER = -2000000000.0
 ANY = pl.BlockSpec(memory_space=pl.ANY)
 VMEM = pl.BlockSpec(memory_space=pltpu.VMEM)
 SMEM = pl.BlockSpec(memory_space=pltpu.SMEM)
@@ -429,11 +429,11 @@
 
 
 class Part:
-    def __init__(self, place, orders, both, core_got, got, final, send_sem, recv_sem):
+    def __init__(self, place, orders, folds, both, core_got, got, final, send_sem, recv_sem):
         self.place, self.orders, self.both = place, orders, both
         self.core_got, self.got, self.final = core_got, got, final
         self.send_sem, self.recv_sem = send_sem, recv_sem
-        self.folds = max(len(order) for order in orders)
+        self.folds = folds
 
     def blocks(self, core, phase, value):
         choices = {}
@@ -582,34 +582,34 @@
         return pltpu.make_async_copy(self.parts[n].final, self.outs[n], self.out_sem.at[n])
 
 
+LN_TWO = 0.6931471805599453
+QUERY_SCALE = HEAD_WIDTH ** (-0.5) / LN_TWO
 TILES = 3
 LASTS = 4
 PIECES = TILES + LASTS
 ORDERS = (
-    ("abxy", "yxz", False),
-    ("yxab", "xzy", False),
-    ("yxz", "yaxb", False),
-    ("yxab", "xyab", True),
-    ("yxab", "xyab", True),
-    ("yxab", "xyab", True),
-    ("yxab", "ayxb", True),
+    (('yxab', 'zxy', 'xyz', 'zyx'), False),
+    (('yxab', 'ayxb', 'xyz', 'yxz'), False),
+    (('xyz', 'yaxb', 'yzx', 'abyx'), False),
+    (('yabx', 'xaby'), False),
+    (('yzx', 'xyz'), False),
+    (('yxab', 'xayb'), True),
+    (('yxz', 'xyz'), True),
 )
 HOOKS = {
     "tile1.1": (0,),
     "tile2.1": (1,),
-    "after0": (0,),
-    "after1": (2,),
-    "far": (1,),
-    "near0": (0,),
-    "near4": (3,),
-    "near5": (4,),
-    "near6": (2,),
-    "last2": (3,),
-    "last3": (1, 5),
-    "into": (6, 4, 0, 2),
+    "after2": (2,),
+    "far": (0, 1),
+    "near3": (2,),
+    "near4": (0, 3, 4),
+    "near5": (1,),
+    "last2": (3, 2),
+    "last3": (5,),
+    "into": (0, 6, 4),
     "norm": (1,),
 }
-TAIL = (3, 5, 4, 6, 2, 0, 1, 5, 3, 6, 4, 2, 5, 0, 3, 1, 6, 4, 1, 0, 5, 2, 3, 6, 4, 2, 5, 6)
+TAIL = (5, 3, 2, 0, 6, 5, 4, 0, 1, 6, 0, 5, 3, 2, 4, 1, 3, 1, 6, 2, 5, 4, 3, 2, 4, 3, 6, 5)
 
 def main_kernel(
     count, tokens, cotangent, qkv_weight, out_weight, up_weight, down_weight,
@@ -666,7 +666,8 @@
         parts = [
             Part(
                 place,
-                ORDERS[n][:2],
+                ORDERS[n][0][2 * which : 2 * which + 2],
+                max(len(order) for order in ORDERS[n][0]),
                 both.at[n],
                 core_got.at[n],
                 got.at[n],
@@ -681,11 +682,12 @@
                 )
             )
         ]
-        pieces.append(Piece(parts, ORDERS[n][2], (down_sums.at[n], up_sums.at[n]), out_sem.at[n]))
+        pieces.append(Piece(parts, ORDERS[n][1], (down_sums.at[n], up_sums.at[n]), out_sem.at[n]))
     for n in range(LASTS):
         part = Part(
             place,
-            ORDERS[TILES + n][:2],
+            ORDERS[TILES + n][0],
+            max(len(order) for order in ORDERS[TILES + n][0]),
             last_both.at[n],
             last_core.at[n],
             last_got.at[n],
@@ -693,7 +695,7 @@
             send_sem.at[TILES + n, 0],
             recv_sem.at[TILES + n, 0],
         )
-        pieces.append(Piece([part], ORDERS[TILES + n][2], (last_sums.at[n],), out_sem.at[TILES + n]))
+        pieces.append(Piece([part], ORDERS[TILES + n][1], (last_sums.at[n],), out_sem.at[TILES + n]))
 
     def hook(name):
         for n in HOOKS.get(name, ()):
@@ -741,12 +743,13 @@
                     send, recv = gather_send_sem.at[n], gather_recv_sem.at[n]
                     remote(mine, mine, send, recv, peer).start()
         landed(3).wait()
-        projected = (nn(h1[...], wqkv[0]) * HEAD_WIDTH ** (-0.5)).astype(LOW)
+        projected = (nn(h1[...], wqkv[0]) * QUERY_SCALE).astype(LOW)
         query[:, :HEAD_WIDTH, :] = projected.T.reshape(HEADS, HEAD_WIDTH, rows)
         places = lax.broadcasted_iota(jnp.int32, (1, rows), 1)
         places = first_row + (places % chosen) * DILATION_STEP + places // chosen
         mask_rows(key, jnp.where(places < limit, 0.0, NEVER))
         mask_rows(query, jnp.ones((1, rows), FULL))
+        mask_rows(value, jnp.ones((1, rows), FULL))
 
         @pl.loop(0, HEADS // members)
         def _(group):
@@ -760,12 +763,12 @@
                 head = group * members + member
                 scores = tn(key[head], query[head])
                 highest = jnp.max(scores, axis=0, keepdims=True)
-                exponent = jnp.exp(scores - highest)
+                low = jnp.exp2(scores - highest).astype(LOW)
                 top[head] = highest
-                total[head] = jnp.sum(exponent, axis=0, keepdims=True)
-                low = exponent.astype(LOW)
                 weights[group % 2, member] = low
-                attended[head] = nn(value[head], low)
+                result = nn(value[head], low)
+                attended[head] = result[:HEAD_WIDTH]
+                total[head] = result[HEAD_WIDTH : HEAD_WIDTH + 1]
             pltpu.make_async_copy(slot, kept, sem).start()
 
         normed[...] = h1[...].T
@@ -789,6 +792,7 @@
             ref[:, :HEAD_WIDTH, :] = projected.T.reshape(HEADS, HEAD_WIDTH, distant)
         places = lax.broadcasted_iota(jnp.int32, (1, distant), 1) * DILATION_STEP
         mask_rows(far_key, jnp.where(places < limit, 0.0, NEVER))
+        mask_rows(far_value, jnp.ones((1, distant), FULL))
         lane_mask = jnp.where(lax.broadcasted_iota(jnp.int32, (1, LANES), 1) < chosen, 0.0, NEVER)
 
         @pl.loop(0, HEADS // 4)
@@ -797,21 +801,20 @@
                 head = group * 4 + member
                 scores = tn(far_key[head], query[head][:, :LANES]) + lane_mask
                 highest = jnp.max(scores, axis=0, keepdims=True)
-                exponent = jnp.exp(scores - highest)
-                low = exponent.astype(LOW)
+                low = jnp.exp2(scores - highest).astype(LOW)
                 far_weights[head] = low
                 near = top[head][:, :LANES]
                 joint = jnp.maximum(near, highest)
-                near_part, far_part = jnp.exp(near - joint), jnp.exp(highest - joint)
-                joint_total = total[head][:, :LANES] * near_part + far_part * jnp.sum(
-                    exponent, axis=0, keepdims=True
-                )
+                near_part, far_part = jnp.exp2(near - joint), jnp.exp2(highest - joint)
+                far_result = nn(far_value[head], low)
+                far_total = far_result[HEAD_WIDTH : HEAD_WIDTH + 1]
+                joint_total = total[head][:, :LANES] * near_part + far_total * far_part
                 near_part, far_part = near_part / joint_total, far_part / joint_total
                 far_scale[head] = far_part
                 local = jnp.concatenate([near_part, 1.0 / total[head][:, LANES:]], axis=1)
                 scale[head] = local
                 result = attended[head] * local
-                with_far = result[:, :LANES] + nn(far_value[head], low) * far_part
+                with_far = result[:, :LANES] + far_result[:HEAD_WIDTH] * far_part
                 result = jnp.concatenate([with_far, result[:, LANES:]], axis=1)
                 attn[head] = result.astype(LOW)
 
@@ -873,18 +876,13 @@
             @pl.loop(0, halves)
             def _(half, tile=tile):
                 wait_tile(half)
-                for part in range(2):
-                    at = slice(part * per_half // 2, (part + 1) * per_half // 2)
-                    to = pl.ds(
-                        pl.multiple_of(half * per_half + part * per_half // 2, LANES), per_half // 2
-                    )
-                    hidden = nn(h2[...], wup[half, :, at])
-                    hidden_slope = nt(dyb[...], wdown[half, at])
-                    share = 0.5 * (1.0 + lax.erf(hidden * 0.7071067811865476))
-                    active[:, to] = (hidden * share).astype(LOW)
-                    density = hidden * jnp.exp(-0.5 * hidden * hidden) * 0.3989422804014327
-                    low_slope[:, to] = (hidden_slope * (share + density)).astype(LOW)
                 to = pl.ds(pl.multiple_of(half * per_half, LANES), per_half)
+                hidden = nn(h2[...], wup[half])
+                hidden_slope = nt(dyb[...], wdown[half])
+                share = 0.5 * (1.0 + lax.erf(hidden * 0.7071067811865476))
+                active[:, to] = (hidden * share).astype(LOW)
+                density = hidden * jnp.exp(-0.5 * hidden * hidden) * 0.3989422804014327
+                low_slope[:, to] = (hidden_slope * (share + density)).astype(LOW)
                 after[...] += nn(active[:, to], wdown[half])
                 resid[...] += nt(low_slope[:, to], wup[half])
                 if tile + 1 < TILES:
@@ -970,11 +968,12 @@
                 head = group * 4 + member
                 first_slope = slope[head][:, :LANES]
                 low = far_weights[head]
-                change = tn(far_value[head], first_slope) - delta[head][:, :LANES]
+                change = tn(far_value[head, :HEAD_WIDTH], first_slope) - delta[head][:, :LANES]
                 score_slope = (low.astype(FULL) * far_scale[head] * change).astype(LOW)
                 far_query[head] = nn(far_key[head, :HEAD_WIDTH], score_slope)
                 scaled = (first_slope.astype(FULL) * far_scale[head]).astype(LOW)
-                given[0, head] = nt(query[head, :HEAD_WIDTH, :LANES], score_slope).astype(LOW)
+                key_slope = nt(query[head, :HEAD_WIDTH, :LANES], score_slope)
+                given[0, head] = (key_slope * LN_TWO).astype(LOW)
                 given[1, head] = nt(scaled, low).astype(LOW)
 
         hook("far0")
@@ -1005,7 +1004,7 @@
             for member in range(members):
                 head = group * members + member
                 low = weights[group % 2, member]
-                change = tn(value[head], slope[head]) - delta[head]
+                change = tn(value[head, :HEAD_WIDTH], slope[head]) - delta[head]
                 score_slope = (low.astype(FULL) * scale[head] * change).astype(LOW)
                 query_slope = nn(key[head, :HEAD_WIDTH], score_slope)
                 key_slope = nt(query[head, :HEAD_WIDTH], score_slope)
@@ -1014,7 +1013,7 @@
                 first = query_slope[:, :LANES] + far_query[head]
                 query_slope = jnp.concatenate([first, query_slope[:, LANES:]], axis=1)
                 slopes[0, head] = (query_slope * HEAD_WIDTH ** (-0.5)).astype(LOW)
-                slopes[1, head] = key_slope.astype(LOW)
+                slopes[1, head] = (key_slope * LN_TWO).astype(LOW)
                 slopes[2, head] = value_slope.astype(LOW)
                 if member % 2:
                     hook("near%d" % (head // 2))
@@ -1115,7 +1114,7 @@
     blocks = ((TILES, down_block), (TILES, up_block), (LASTS, last_block))
     low = [
         (width, rows), (width, distant), (HEADS, AUG, rows), (HEADS, AUG, rows),
-        (HEADS, HEAD_WIDTH, rows), (HEADS, AUG, distant), (HEADS, HEAD_WIDTH, distant),
+        (HEADS, AUG, rows), (HEADS, AUG, distant), (HEADS, AUG, distant),
         (HEADS, distant, LANES),
     ]
     scratch = [vm(shape, LOW) for shape in low]

time: 123 us -> 120 us (0.976)
  Pallas kernels: 121 us -> 118 us
    pallas_call x1, Pallas kernels: 117 us -> 114 us  [main_pass(): pl.pallas_call(functools.partial(main_kernel, count), out_shape=(jax.Shap...]
where the time goes in v1:
time: 120 us; the launch traced here: 119 us
  Pallas kernels  118 us (98%)
  between operations  1.48 us (1%)
    pallas_call x1, Pallas kernels, main_pass(): pl.pallas_call(functools.partial(main_kernel, count), out_shape=(jax.Shap...  114 us
    pallas_call x1, Pallas kernels, finish_pass(): pl.pallas_call(finish_kernel, out_shape=(jax.ShapeDtypeStruct((rows, widt...  4.14 us

profile of v1, /device:TPU:0, one launch (start us, length us, event | category | flops | bytes accessed | tf_op | source)
XLA Modules:
  0.0 119.5 jit_solution(7349128694904386226)
XLA Ops:
  1.3 113.9 %main_pass.1 = (bf16[512,768]{1,0:T(8,128)(2,1)}, bf16[512,768]{1,0:T(8,128)(2,1)}, bf16[3,4,32,768]{3,2,1,0:T(8,128)(2,1)}, bf16[3,4,96,256]{3,2,1,0:T(8,128)(2...) custom-call(bf16[512,768]{1,0:T(8,128)(2,1)} %bitcast.4, ...), custom_call_target="tpu_custom_call" | custom-call | tf_op jit(solution)/shard_map/main_pass/pallas_call | solution.py:1152
  115.2 4.1 %finish_pass.1 = (bf16[512,768]{1,0:T(8,128)(2,1)}, bf16[512,768]{1,0:T(8,128)(2,1)}, f32[96,2304]{1,0:T(8,128)}, f32[96,768]{1,0:T(8,128)}, f32[96,3072]{1,0:T(...) custom-call(bf16[512,768]{1,0:T(8,128)(2,1)} %get-tuple-element.26.mixed, ...), custom_call_target="tpu_custom_call" | custom-call | tf_op jit(solution)/shard_map/finish_pass/pallas_call | solution.py:1254

commit v2 on v1

--- a/solution.py
+++ b/solution.py
@@ -582,6 +582,7 @@
         return pltpu.make_async_copy(self.parts[n].final, self.outs[n], self.out_sem.at[n])
 
 
+EARLY = 5
 LN_TWO = 0.6931471805599453
 QUERY_SCALE = HEAD_WIDTH ** (-0.5) / LN_TWO
 TILES = 3
@@ -609,7 +610,7 @@
     "into": (0, 6, 4),
     "norm": (1,),
 }
-TAIL = (5, 3, 2, 0, 6, 5, 4, 0, 1, 6, 0, 5, 3, 2, 4, 1, 3, 1, 6, 2, 5, 4, 3, 2, 4, 3, 6, 5)
+TAIL = (5, 3, 2, 0, 6, 5, 0, 4, 1, 6, 0, 5, 3, 2, 4, 1, 3, 1, 6, 2, 5, 3, 2, 4, 3, 6, 4, 5)
 
 def main_kernel(
     count, tokens, cotangent, qkv_weight, out_weight, up_weight, down_weight,
@@ -1032,6 +1033,9 @@
         pltpu.make_async_copy(staged, mixed_out, store_sem.at[1]).wait()
         spread(wide, into.T)
         hook("into")
+        hook("norm")
+        for n in TAIL[:EARLY]:
+            pieces[n].advance()
         total = far_send[seq].astype(FULL)
         for n in range(count - 1):
             wait = remote(
@@ -1067,8 +1071,6 @@
     for n, peer in enumerate(peers):
         mine = around.at[seq]
         remote(mine, mine, norm_send_sem.at[n], norm_recv_sem.at[n], peer).start()
-    hook("norm")
-
     @steps
     def _(step):
         strided_store(wide, step, chosen, resid[chunk(step, chosen)])
@@ -1089,7 +1091,7 @@
     for n, peer in enumerate(place.slide_peers):
         mine, at = across.at[place.slide], count - 1 + n
         remote(mine, mine, norm_send_sem.at[at], norm_recv_sem.at[at], peer).start()
-    for n in TAIL + tuple(range(PIECES)) * 6:
+    for n in TAIL[EARLY:] + tuple(range(PIECES)) * 6:
         pieces[n].advance()
     for n in range(3):
         mine, at = across.at[0], count - 1 + n

time: 120 us -> 120 us (level)
  no operation moved by 1% of the time
where the time goes in v2:
time: 120 us; the launch traced here: 119 us
  Pallas kernels  118 us (98%)
  between operations  1.48 us (1%)
    pallas_call x1, Pallas kernels, main_pass(): pl.pallas_call(functools.partial(main_kernel, count), out_shape=(jax.Shap...  114 us
    pallas_call x1, Pallas kernels, finish_pass(): pl.pallas_call(finish_kernel, out_shape=(jax.ShapeDtypeStruct((rows, widt...  4.14 us

profile of v2, /device:TPU:0, one launch (start us, length us, event | category | flops | bytes accessed | tf_op | source)
XLA Modules:
  0.0 119.4 jit_solution(16413705548799695922)
XLA Ops:
  1.3 113.7 %main_pass.1 = (bf16[512,768]{1,0:T(8,128)(2,1)}, bf16[512,768]{1,0:T(8,128)(2,1)}, bf16[3,4,32,768]{3,2,1,0:T(8,128)(2,1)}, bf16[3,4,96,256]{3,2,1,0:T(8,128)(2...) custom-call(bf16[512,768]{1,0:T(8,128)(2,1)} %bitcast.4, ...), custom_call_target="tpu_custom_call" | custom-call | tf_op jit(solution)/shard_map/main_pass/pallas_call | solution.py:1154
  115.0 4.1 %finish_pass.1 = (bf16[512,768]{1,0:T(8,128)(2,1)}, bf16[512,768]{1,0:T(8,128)(2,1)}, f32[96,2304]{1,0:T(8,128)}, f32[96,768]{1,0:T(8,128)}, f32[96,3072]{1,0:T(...) custom-call(bf16[512,768]{1,0:T(8,128)(2,1)} %get-tuple-element.26.mixed, ...), custom_call_target="tpu_custom_call" | custom-call | tf_op jit(solution)/shard_map/finish_pass/pallas_call | solution.py:1256
